TPU v7x, 512 devices: a whole 4x8x8 slice. The times are simulated.
512 devices in a mesh: cfg: 2 (over y_hi), seq: 32 (over z, y_lo), blk: 8 (over x, core).
Axes of the slice: x: 4, y: 8 (y_hi: 2, y_lo: 4; y = y_hi * 4 + y_lo), z: 8, core: 2. Of those that a mesh axis runs over, the one named last changes fastest.
Arguments:
- tokens_in: bfloat16 [2, 4096, 1536], P('cfg', 'seq'), may hold values from -6 to 6
- modulation: float32 [2, 8, 1536], replicated, may hold values from -3 to 3
- qk_gain: float32 [2, 64], replicated, as said below
- qkv_weight: bfloat16 [3, 1536, 1536], P(None, 'blk'), may hold values from -0.15625 to 0.15625
- out_weight: bfloat16 [1536, 1536], P('blk'), may hold values from -0.15625 to 0.15625
- up_weight: bfloat16 [1536, 6144], P('seq', 'blk'), may hold values from -0.15625 to 0.15625
- down_weight: bfloat16 [6144, 1536], P('blk', 'seq'), may hold values from -0.078125 to 0.078125
- proj_weight: bfloat16 [1536, 64], replicated, may hold values from -0.15625 to 0.15625
- latent: float32 [4096, 64], P(('seq', 'blk'), 'cfg'), may hold values from -6 to 6
- text_count: int32 [1], replicated, may hold values from 64 to 2047
- positions: int32 [3, 4096], P(None, 'seq'), may hold values from 0 to 47
- step_index: int32 [1], replicated, may hold values from 20 to 999
- guidance: float32 [1], replicated, may hold values from 4 to 8
Outputs:
- hidden_out: bfloat16 [2, 4096, 1536], P('cfg', ('seq', 'blk'))
- latent_prev: float32 [4096, 64], P(('seq', 'blk'), 'cfg')
Inputs may be any that keep to these rules, and one draw needn't show every extreme that they name: `qk_gain`: positive gains.
All inputs are finite; a program needn't handle non-finite values.
Results may differ from a plain program's by a relative error of at most 0.015.
The roundings to bfloat16 on the way count: a program that leaves them out, or rounds other values in their place, can miss the bound.
Values may be sent and summed in bfloat16 or wider, within the bound.
No kernel may reach another device: no remote copies, remote signals or barrier semaphores. Data moves between devices by JAX's collectives and lax.ppermute only.
A program may use at most 64 MiB of HBM per device.

v0:
```python
import math
import jax
import jax.numpy as jnp
from jax import lax
from jax.sharding import PartitionSpec as P

HEAD = 64
STRIDE = 20
rope_bands = (16, 24, 24)


def swapped(block, axis, stride):
    count = lax.axis_size(axis)
    route = []
    for low in range(count):
        high = low | 1 << stride
        if high != low and high < count:
            route += [(low, high), (high, low)]
    return lax.ppermute(block, axis, route)


def layer_norm(values, epsilon):
    average = jnp.mean(values, -1, keepdims=True)
    centered = values - average
    spread = jnp.mean(centered * centered, -1, keepdims=True)
    return centered * lax.rsqrt(spread + epsilon)


def pick_mods(modulation, is_video, which):
    return jnp.where(
        is_video[:, None], modulation[1, which][None, :], modulation[0, which][None, :]
    )


def modulate(values, modulation, is_video, shift_row, scale_row):
    normed = layer_norm(values, 1e-05)
    return normed * (1.0 + pick_mods(modulation, is_video, scale_row)) + pick_mods(
        modulation, is_video, shift_row
    )


def rope_tables(positions, is_video):
    angle_parts = []
    for axis_pos, band_width in enumerate(rope_bands):
        exponent = jnp.arange(band_width // 2, dtype=jnp.float32) * (2.0 / band_width)
        inverse = jnp.exp(-exponent * math.log(10000.0))
        angle_parts.append(positions[axis_pos].astype(jnp.float32)[:, None] * inverse[None, :])
    angles = jnp.concatenate(angle_parts, 1) * is_video.astype(jnp.float32)[:, None]
    return (jnp.cos(angles), jnp.sin(angles))


def rotate(vectors, cosine, sine):
    pieces = []
    offset = 0
    half_offset = 0
    for band_width in rope_bands:
        half_width = band_width // 2
        first_half = vectors[..., offset : offset + half_width]
        second = vectors[..., offset + half_width : offset + band_width]
        cos_band = cosine[:, None, half_offset : half_offset + half_width]
        sin_band = sine[:, None, half_offset : half_offset + half_width]
        pieces.append(first_half * cos_band - second * sin_band)
        pieces.append(second * cos_band + first_half * sin_band)
        offset = offset + band_width
        half_offset = half_offset + half_width
    return jnp.concatenate(pieces, -1)


def head_prep(flat_heads, gain, cosine, sine):
    token_count = flat_heads.shape[0]
    shaped = flat_heads.reshape(token_count, -1, HEAD)
    normed = layer_norm(shaped, 1e-06) * gain[None, None, :]
    turned = rotate(normed, cosine, sine)
    return turned.reshape(token_count, -1).astype(jnp.bfloat16)


def ddim_update(latent, guided, step_index):
    steps_all = jnp.arange(1000, dtype=jnp.float32)
    root_beta = math.sqrt(0.00085) + steps_all / 999.0 * (math.sqrt(0.012) - math.sqrt(0.00085))
    alpha_bar = jnp.exp(jnp.cumsum(jnp.log1p(-root_beta * root_beta)))
    indices = jnp.arange(1000, dtype=jnp.int32)
    alpha_now = jnp.sum(jnp.where(indices == step_index[0], alpha_bar, 0.0))
    alpha_prev = jnp.sum(jnp.where(indices == step_index[0] - STRIDE, alpha_bar, 0.0))
    clean_est = jnp.sqrt(alpha_now) * latent - jnp.sqrt(1.0 - alpha_now) * guided
    noise_est = jnp.sqrt(1.0 - alpha_now) * latent + jnp.sqrt(alpha_now) * guided
    return jnp.sqrt(alpha_prev) * clean_est + jnp.sqrt(1.0 - alpha_prev) * noise_est


def body(
    tokens_in,
    modulation,
    qk_gain,
    qkv_weight,
    out_weight,
    up_weight,
    down_weight,
    proj_weight,
    latent,
    text_count,
    positions,
    step_index,
    guidance,
):
    row_count = tokens_in.shape[1]
    own_count = row_count // lax.axis_size("blk")
    blk_index = lax.axis_index("blk")
    token_ids = lax.axis_index("seq") * row_count + jnp.arange(row_count, dtype=jnp.int32)
    is_video = token_ids >= text_count[0]
    own_video = lax.dynamic_slice_in_dim(is_video, blk_index * own_count, own_count, 0)
    residual = tokens_in[0].astype(jnp.float32)
    cosine, sine = rope_tables(positions, is_video)
    normed = modulate(residual, modulation, is_video, 0, 1).astype(jnp.bfloat16)
    projected = jnp.einsum("td,ked->kte", normed, qkv_weight, preferred_element_type=jnp.float32)
    head_count = projected.shape[2] // HEAD
    queries = head_prep(projected[0], qk_gain[0], cosine, sine)
    keys_local = head_prep(projected[1], qk_gain[1], cosine, sine)
    values_local = projected[2].astype(jnp.bfloat16)
    query_heads = queries.reshape(row_count, head_count, HEAD)
    initial = (
        jnp.full((head_count, row_count), -1e30, jnp.float32),
        jnp.zeros((head_count, row_count), jnp.float32),
        jnp.zeros((head_count, row_count, HEAD), jnp.float32),
    )
    key_piece = lax.all_gather(keys_local, "seq", axis=0, tiled=True)
    value_piece = lax.all_gather(values_local, "seq", axis=0, tiled=True)
    piece_len = key_piece.shape[0]
    key_blocks = key_piece.reshape(piece_len // piece_len, piece_len, head_count, HEAD)
    value_blocks = value_piece.reshape(piece_len // piece_len, piece_len, head_count, HEAD)

    def absorb_block(state, key_value):
        key_block, value_block = key_value
        running_max, running_sum, weighted = state
        scores = (
            jnp.einsum("thd,shd->hts", query_heads, key_block, preferred_element_type=jnp.float32)
            * 0.125
        )
        new_max = jnp.maximum(running_max, jnp.max(scores, -1))
        rescale = jnp.exp(running_max - new_max)
        weights = jnp.exp(scores - new_max[..., None])
        running_sum = running_sum * rescale + jnp.sum(weights, -1)
        weighted = weighted * rescale[..., None] + jnp.einsum(
            "hts,shd->htd",
            weights.astype(jnp.bfloat16),
            value_block,
            preferred_element_type=jnp.float32,
        )
        return ((new_max, running_sum, weighted), None)

    state, unused = lax.scan(absorb_block, initial, (key_blocks, value_blocks))
    running_max, running_sum, weighted = state
    attn_out = (
        (weighted / running_sum[..., None])
        .transpose(1, 0, 2)
        .reshape(row_count, head_count * HEAD)
        .astype(jnp.bfloat16)
    )
    attn_proj = lax.psum(
        jnp.dot(attn_out, out_weight, preferred_element_type=jnp.float32).astype(jnp.bfloat16),
        "blk",
    ).astype(jnp.float32)
    after_attn = residual + pick_mods(modulation, is_video, 2) * attn_proj
    normed_mlp = modulate(after_attn, modulation, is_video, 3, 4).astype(jnp.bfloat16)
    own_after = lax.dynamic_slice_in_dim(after_attn, blk_index * own_count, own_count, 0)
    up_full, down_full = (
        lax.all_gather(up_weight, "seq", axis=0, tiled=True),
        lax.all_gather(down_weight, "seq", axis=1, tiled=True),
    )
    hidden_up = jnp.dot(normed_mlp, up_full, preferred_element_type=jnp.float32)
    activated = jax.nn.gelu(hidden_up, approximate=True).astype(jnp.bfloat16)
    mlp_part = jnp.dot(activated, down_full, preferred_element_type=jnp.float32)
    mlp_rows = lax.psum_scatter(
        mlp_part.astype(jnp.bfloat16), "blk", scatter_dimension=0, tiled=True
    ).astype(jnp.float32)
    after_mlp = own_after + pick_mods(modulation, own_video, 5) * mlp_rows
    hidden_out = after_mlp.astype(jnp.bfloat16)[None]
    final_norm = modulate(after_mlp, modulation, own_video, 6, 7).astype(jnp.bfloat16)
    predicted = jnp.dot(final_norm, proj_weight, preferred_element_type=jnp.float32)
    half_width = latent.shape[1]
    branch_index = lax.axis_index("cfg")
    kept = lax.dynamic_slice_in_dim(predicted, branch_index * half_width, half_width, 1)
    outgoing = lax.dynamic_slice_in_dim(predicted, (1 - branch_index) * half_width, half_width, 1)
    partner = swapped(outgoing, "cfg", 0)
    is_cond = branch_index == 0
    cond_pred = jnp.where(is_cond, kept, partner)
    uncond_pred = jnp.where(is_cond, partner, kept)
    guided = uncond_pred + guidance[0] * (cond_pred - uncond_pred)
    latent_prev = ddim_update(latent, guided, step_index)
    return (hidden_out, latent_prev)


def solution(mesh):
    in_specs = (
        P("cfg", "seq", None),
        P(),
        P(),
        P(None, "blk", None),
        P("blk", None),
        P("seq", "blk"),
        P("blk", "seq"),
        P(),
        P(("seq", "blk"), "cfg"),
        P(),
        P(None, "seq"),
        P(),
        P(),
    )
    out_specs = (P("cfg", ("seq", "blk"), None), P(("seq", "blk"), "cfg"))
    return jax.shard_map(body, mesh=mesh, in_specs=in_specs, out_specs=out_specs, check_vma=False)
```

profile of v0, /device:TPU:64, one launch (start us, length us, event | category | flops | bytes accessed | tf_op | source)
XLA Modules:
  0.0 744.4 jit_solution(7766577091344267166)
XLA Ops:
  7.2 0.0 copy-start
  7.2 0.0 all-gather.6.cloned.1.call-start
  8.0 0.8 convert_bitcast_fusion.4
  8.8 0.1 broadcast_multiply_fusion.2
  8.9 0.1 broadcast_multiply_fusion.1
  9.0 0.1 fusion.74
  9.1 1.8 slice_reduce_fusion.3
  10.9 1.1 convert_reduce_fusion
  12.0 0.0 copy-start.5
  12.0 1.3 fusion.21
  13.3 0.0 copy-done
  13.3 1.7 convolution_bitcast_fusion
  15.3 0.0 copy-done.5
  15.3 0.1 multiply_multiply_fusion.1
  15.4 5.1 concatenate.13
  20.5 0.0 all-gather.6.cloned.1.call-update
  20.5 0.0 all-gather.12.cloned.1.call-start
  20.6 0.6 slice.262
  21.2 0.1 all-gather.12.cloned.1.call-update
  21.3 0.0 all-reduce.3.cloned.1.call-start
  21.4 0.3 concatenate.12
  21.7 134.0 %all-gather.6.cloned.1.call-done = bf16[4096,192]{0,1:T(8,128)(2,1)} async-done(((bf16[128,192]{0,1:T(8,128)(2,1)}), bf16[4096,192]{0,1:T(8,128)(2,1)}) %all-gather.6.cloned.1.call-update) | async-done | bytes 1572880 | tf_op jit(solution)/shard_map/all_gather | solution.py:124
  155.6 2.5 fusion.90
  158.1 0.0 copy-start.1
  158.2 1.0 fusion
  159.1 1.7 copy-done.1
  160.8 124.8 %all-gather.12.cloned.1.call-done = bf16[1,4096,192]{1,2,0:T(8,128)(2,1)} async-done(((bf16[1,128,192]{1,2,0:T(8,128)(2,1)}), bf16[1,4096,192]{1,2,0:T(8,128)(2,1)}) %all-gather.12.cloned.1.call-update) | async-done | bytes 1572880 | tf_op jit(solution)/shard_map/all_gather | solution.py:125
  285.6 0.0 copy-start.3
  285.6 0.0 copy-start.2
  285.6 4.6 fusion.14
  290.3 0.0 copy-done.3
  290.3 1.1 convolution_convert_fusion.1
  291.3 0.0 all-reduce.3.cloned.1.call-update
  291.3 0.0 all-gather.10.cloned.1.call-start
  291.4 0.5 all-gather.10.cloned.1.call-update
  291.9 0.0 all-gather.8.cloned.1.call-start
  292.0 0.5 all-gather.8.cloned.1.call-update
  292.5 0.0 reduce-scatter.2.cloned.1.call-start
  292.6 66.6 %all-reduce.3.cloned.1.call-done = bf16[128,1536]{1,0:T(8,128)(2,1)} async-done(((bf16[128,1536]{1,0:T(8,128)(2,1)}), bf16[128,1536]{1,0:T(8,128)(2,1)}) %all-reduce.3.cloned.1.call-update) | async-done | bytes 393232 | tf_op jit(solution)/shard_map/psum | solution.py:157
  359.1 0.0 copy-done.2
  359.1 1.3 fusion.84
  360.4 0.2 multiply_reduce_fusion
  360.7 154.4 %all-gather.10.cloned.1.call-done = bf16[768,1536]{0,1:T(8,128)(2,1)} async-done(((bf16[768,48]{0,1:T(8,128)(2,1)}), bf16[768,1536]{0,1:T(8,128)(2,1)}) %all-gather.10.cloned.1.call-update) | async-done | bytes 2359312 | tf_op jit(solution)/shard_map/all_gather | solution.py:166
  515.1 162.1 %all-gather.8.cloned.1.call-done = bf16[1536,768]{1,0:T(8,128)(2,1)} async-done(((bf16[48,768]{1,0:T(8,128)(2,1)}), bf16[1536,768]{1,0:T(8,128)(2,1)}) %all-gather.8.cloned.1.call-update) | async-done | bytes 2359312 | tf_op jit(solution)/shard_map/all_gather | solution.py:165
  677.3 0.0 copy-start.6
  677.3 0.0 copy-start.4
  677.3 4.5 convolution_convert_fusion
  681.8 0.0 reduce-scatter.2.cloned.1.call-update
  681.8 0.1 dynamic_slice.18
  681.9 0.3 reduce-window.9
  682.2 0.1 slice.181
  683.0 0.1 slice_reduce_fusion.16
  683.1 0.1 add_bitcast_fusion
  683.1 40.3 %reduce-scatter.2.cloned.1.call-done = bf16[16,1536]{1,0:T(8,128)(2,1)} async-done(((bf16[128,1536]{1,0:T(8,128)(2,1)}), bf16[16,1536]{1,0:T(8,128)(2,1)}) %reduce-scatter.2.cloned.1.call-update) | async-done | bytes 49168 | tf_op jit(solution)/shard_map/reduce_scatter | solution.py:171
  723.4 1.0 fusion.83
  724.4 0.7 multiply_reduce_fusion.1
  725.2 0.0 copy-done.6
  725.2 0.2 fusion.64
  725.4 0.1 constant_dynamic-slice_fusion
  725.5 7.4 collective-permute-start
  732.9 0.7 select_reduce_fusion
  736.9 0.0 collective-permute-done
  736.9 0.0 copy-done.4
  736.9 0.7 multiply_add_fusion.1
  (30 shorter events, 0.4 us)
Async XLA Ops:
  7.2 6.2 copy-start
  7.2 148.4 %all-gather.6.cloned.1.call-start = ((), (), s32[]{:S(2)}) async-start(), calls=%async_computation.1 | async-start | bytes 1622016 | tf_op jit(solution)/shard_map/all_gather | solution.py:124
  12.0 3.2 copy-start.5
  20.5 265.1 %all-gather.12.cloned.1.call-start = ((), (), s32[]{:S(2)}) async-start(), calls=%async_computation.6 | async-start | bytes 1622016 | tf_op jit(solution)/shard_map/all_gather | solution.py:125
  21.3 337.8 %all-reduce.3.cloned.1.call-start = ((), (), s32[]{:S(2)}) async-start(), calls=%async_computation.2 | async-start | bytes 786432 | tf_op jit(solution)/shard_map/psum | solution.py:157
  158.1 2.7 copy-start.1
  285.6 4.6 copy-start.3
  285.6 73.5 %copy-start.2 = (bf16[1,128,1536]{2,1,0:T(8,128)(2,1)S(1)}, bf16[1,128,1536]{2,1,0:T(8,128)(2,1)}, u32[]{:S(2)}) copy-start(bf16[1,128,1536]{2,1,0:T(8,128)(2,1)} %param.13) | copy-start | bytes 1179652
  291.3 223.8 %all-gather.10.cloned.1.call-start = ((), (), s32[]{:S(2)}) async-start(), calls=%async_computation.4 | async-start | bytes 2433024 | tf_op jit(solution)/shard_map/all_gather | solution.py:166
  291.9 385.3 %all-gather.8.cloned.1.call-start = ((), (), s32[]{:S(2)}) async-start(), calls=%async_computation.3 | async-start | bytes 2433024 | tf_op jit(solution)/shard_map/all_gather | solution.py:165
  292.5 430.9 %reduce-scatter.2.cloned.1.call-start = ((), (), s32[]{:S(2)}) async-start(), calls=%async_computation.5 | async-start | bytes 442368 | tf_op jit(solution)/shard_map/reduce_scatter | solution.py:171
  677.3 47.9 %copy-start.6 = (bf16[1536,64]{0,1:T(8,128)(2,1)S(1)}, bf16[1536,64]{0,1:T(8,128)(2,1)}, u32[]{:S(2)}) copy-start(bf16[1536,64]{0,1:T(8,128)(2,1)} %param.20) | copy-start | bytes 589828
  677.3 59.6 %copy-start.4 = (f32[16,32]{1,0:T(8,128)S(1)}, f32[16,32]{1,0:T(8,128)}, u32[]{:S(2)}) copy-start(f32[16,32]{1,0:T(8,128)} %param.21) | copy-start | bytes 6148
  725.5 11.4 %collective-permute-start = (f32[16,32]{1,0:T(8,128)S(1)}, f32[16,32]{1,0:T(8,128)S(1)}, u32[]{:S(2)}, u32[]{:S(2)}) collective-permute-start(f32[16,32]{1,0:T(8,128)S(1)} %constant_dynamic-slice_fusion), channel_id=1, source_target_pairs={{0,256},{256,0},{1,257},{257,1},{2,258},{258,2},{3,259},{259,3},{4... | collective-permute-start | bytes 6152 | tf_op jit(solution)/shard_map/ppermute | solution.py:19
Sparse Core Ops, SparseCore 0:
  20.7 134.9 all-gather.5
  158.2 127.3 all-gather.11
  291.5 67.6 all-reduce.2
  361.3 153.8 all-gather.9
  517.2 159.9 all-gather.7
  681.9 41.4 reduce-scatter.1
where the time goes:
time: 745 us; the launch traced here: 744 us
  waiting for transfers between devices  683 us (92%)
  between operations  19.1 us (3%)
  matrix products  14.7 us (2%)
  local copies, waits for them, and re-layouts  9.89 us (1%)
  other arithmetic  9.82 us (1%)
  starting transfers between devices  7.61 us (1%)
    all_gather x1, waiting for transfers between devices, body(): lax.all_gather(up_weight, 'seq', axis=0, tiled=True)  162 us
    all_gather x1, waiting for transfers between devices, body(): lax.all_gather(down_weight, 'seq', axis=1, tiled=True)  154 us
    all_gather x1, waiting for transfers between devices, body(): key_piece = lax.all_gather(keys_local, 'seq', axis=0, tiled=True)  134 us
    all_gather x1, waiting for transfers between devices, body(): value_piece = lax.all_gather(values_local, 'seq', axis=0, tiled=True)  125 us
    psum x1, waiting for transfers between devices, body(): lax.psum(jnp.dot(attn_out, out_weight, preferred_element_type=jnp.float32...  66.6 us
    reduce_scatter x1, waiting for transfers between devices, body(): lax.psum_scatter(mlp_part.astype(jnp.bfloat16), 'blk', scatter_dimension=...  40.3 us
  transfers between devices with their start and end apart: 7, of which 6 were waited for; matrix products, arithmetic and copies ran while one was open for 1% of the time, Pallas kernels for 0%

commit v1 on v0

--- a/solution.py
+++ b/solution.py
@@ -121,7 +121,9 @@
         jnp.zeros((head_count, row_count), jnp.float32),
         jnp.zeros((head_count, row_count, HEAD), jnp.float32),
     )
-    key_piece = lax.all_gather(keys_local, "seq", axis=0, tiled=True)
+    key_piece = jnp.concatenate(
+        lax.all_to_all(jnp.stack([keys_local] * lax.axis_size("seq")), "seq", 0, 0), axis=0
+    )
     value_piece = lax.all_gather(values_local, "seq", axis=0, tiled=True)
     piece_len = key_piece.shape[0]
     key_blocks = key_piece.reshape(piece_len // piece_len, piece_len, head_count, HEAD)

time: 745 us -> 634 us (0.85)
  waiting for transfers between devices: 683 us -> 554 us
  starting transfers between devices: 7.61 us -> 20.7 us
    all_gather x1 -> x0, waiting for transfers between devices: 134 us -> none  [body(): key_piece = lax.all_gather(keys_local, 'seq', axis=0, tiled=True)]
    all_to_all x0 -> x1, waiting for transfers between devices: none -> 40.5 us  [body(): lax.all_to_all(jnp.stack([keys_local] * lax.axis_size('seq')), 'seq', 0, 0)]
    all_gather x1, waiting for transfers between devices: 125 us -> 88.1 us  [body(): value_piece = lax.all_gather(values_local, 'seq', axis=0, tiled=True)]
    all_to_all x0 -> x1, starting transfers between devices: none -> 13.2 us  [body(): lax.all_to_all(jnp.stack([keys_local] * lax.axis_size('seq')), 'seq', 0, 0)]
    all_gather x1, waiting for transfers between devices: 154 us -> 162 us  [body(): lax.all_gather(down_weight, 'seq', axis=1, tiled=True)]
    all_gather x1, waiting for transfers between devices: 162 us -> 155 us  [body(): lax.all_gather(up_weight, 'seq', axis=0, tiled=True)]
  transfers between devices with their start and end apart: 7 -> 7, of which waited for: 6 -> 6; matrix products, arithmetic and copies ran while one was open for 1% -> 2% of each run, Pallas kernels for 0% -> 0%
where the time goes in v1:
time: 634 us; the launch traced here: 633 us
  waiting for transfers between devices  554 us (87%)
  starting transfers between devices  20.7 us (3%)
  between operations  19.1 us (3%)
  local copies, waits for them, and re-layouts  15 us (2%)
  matrix products  13.2 us (2%)
  other arithmetic  10.4 us (2%)
    all_gather x1, waiting for transfers between devices, body(): lax.all_gather(down_weight, 'seq', axis=1, tiled=True)  162 us
    all_gather x1, waiting for transfers between devices, body(): lax.all_gather(up_weight, 'seq', axis=0, tiled=True)  155 us
    all_gather x1, waiting for transfers between devices, body(): value_piece = lax.all_gather(values_local, 'seq', axis=0, tiled=True)  88.1 us
    psum x1, waiting for transfers between devices, body(): lax.psum(jnp.dot(attn_out, out_weight, preferred_element_type=jnp.float32...  67.7 us
    all_to_all x1, waiting for transfers between devices, body(): lax.all_to_all(jnp.stack([keys_local] * lax.axis_size('seq')), 'seq', 0, 0)  40.5 us
    reduce_scatter x1, waiting for transfers between devices, body(): lax.psum_scatter(mlp_part.astype(jnp.bfloat16), 'blk', scatter_dimension=...  40.3 us
    all_to_all x1, starting transfers between devices, body(): lax.all_to_all(jnp.stack([keys_local] * lax.axis_size('seq')), 'seq', 0, 0)  13.2 us
  transfers between devices with their start and end apart: 7, of which 6 were waited for; matrix products, arithmetic and copies ran while one was open for 2% of the time, Pallas kernels for 0%

profile of v1, /device:TPU:64, one launch (start us, length us, event | category | flops | bytes accessed | tf_op | source)
XLA Modules:
  0.0 632.9 jit_solution(10879350506995949987)
XLA Ops:
  7.2 0.0 copy-start
  8.0 0.8 convert_bitcast_fusion.4
  8.8 0.0 copy-start.14
  8.8 0.1 broadcast_multiply_fusion.2
  8.9 0.1 broadcast_multiply_fusion.1
  8.9 0.1 fusion.74
  9.1 2.4 slice_reduce_fusion.3
  11.5 1.1 convert_reduce_fusion
  12.6 1.3 fusion.21
  13.9 0.0 copy-done
  13.9 1.7 convolution_bitcast_fusion
  15.7 0.0 copy-done.14
  15.7 0.7 copy-done.4
  16.6 0.1 multiply_multiply_fusion.1
  16.7 0.6 add_convert_fusion.12
  17.3 0.3 concatenate.13
  17.6 1.5 stack.2
  19.1 13.2 %all-to-all-start = ((bf16[32,128,192]{1,2,0:T(8,128)(2,1)}), bf16[32,128,192]{1,2,0:T(8,128)(2,1)S(1)}, u32[]{:S(2)}, u32[]{:S(2)}) async-start(bf16[32,128,192]{1,2,0:T(8,128)(2,1)} %stack.2), calls=%async_computation | async-start | bytes 3145728 | tf_op jit(solution)/shard_map/all_to_all | solution.py:125
  32.3 0.0 all-gather.9.cloned.1.call-start
  32.3 1.5 slice.262
  33.9 0.0 all-gather.9.cloned.1.call-update
  33.9 0.0 all-reduce.3.cloned.1.call-start
  34.0 1.7 concatenate.12
  35.6 40.5 %all-to-all-done = bf16[32,128,192]{1,2,0:T(8,128)(2,1)S(1)} async-done(((bf16[32,128,192]{1,2,0:T(8,128)(2,1)}), bf16[32,128,192]{1,2,0:T(8,128)(2,1)S(1)}, u32[]{:S(2)}, u32[]{:S(2)}) %all-to-all-start) | async-done | bytes 1572896 | tf_op jit(solution)/shard_map/all_to_all | solution.py:125
  76.1 2.2 copy.15
  78.3 2.5 squeeze.25
  80.8 1.1 fusion.90
  81.9 1.0 fusion
  82.9 1.7 copy-done.1
  84.6 88.1 %all-gather.9.cloned.1.call-done = bf16[1,4096,192]{1,2,0:T(8,128)(2,1)} async-done(((bf16[1,128,192]{1,2,0:T(8,128)(2,1)}), bf16[1,4096,192]{1,2,0:T(8,128)(2,1)}) %all-gather.9.cloned.1.call-update) | async-done | bytes 1572880 | tf_op jit(solution)/shard_map/all_gather | solution.py:127
  172.7 4.6 fusion.14
  177.3 1.1 convolution_convert_fusion.1
  178.4 0.0 all-reduce.3.cloned.1.call-update
  178.4 0.0 all-gather.5.cloned.1.call-start
  178.4 0.7 all-gather.5.cloned.1.call-update
  179.1 0.0 all-gather.7.cloned.1.call-start
  179.2 0.5 all-gather.7.cloned.1.call-update
  179.7 0.0 reduce-scatter.2.cloned.1.call-start
  179.8 67.7 %all-reduce.3.cloned.1.call-done = bf16[128,1536]{1,0:T(8,128)(2,1)} async-done(((bf16[128,1536]{1,0:T(8,128)(2,1)}), bf16[128,1536]{1,0:T(8,128)(2,1)}) %all-reduce.3.cloned.1.call-update) | async-done | bytes 393232 | tf_op jit(solution)/shard_map/psum | solution.py:159
  247.4 0.0 copy-done.2
  247.4 1.3 fusion.84
  248.8 0.2 multiply_reduce_fusion
  249.0 154.6 %all-gather.5.cloned.1.call-done = bf16[1536,768]{1,0:T(8,128)(2,1)} async-done(((bf16[48,768]{1,0:T(8,128)(2,1)}), bf16[1536,768]{1,0:T(8,128)(2,1)}) %all-gather.5.cloned.1.call-update) | async-done | bytes 2359312 | tf_op jit(solution)/shard_map/all_gather | solution.py:167
  403.6 162.1 %all-gather.7.cloned.1.call-done = bf16[768,1536]{0,1:T(8,128)(2,1)} async-done(((bf16[768,48]{0,1:T(8,128)(2,1)}), bf16[768,1536]{0,1:T(8,128)(2,1)}) %all-gather.7.cloned.1.call-update) | async-done | bytes 2359312 | tf_op jit(solution)/shard_map/all_gather | solution.py:168
  565.7 0.0 copy-done.9
  565.7 0.0 copy-start.5
  565.8 0.0 copy-start.17
  565.8 0.0 copy-start.13
  565.8 4.5 convolution_convert_fusion
  570.3 0.0 reduce-scatter.2.cloned.1.call-update
  570.4 0.1 dynamic_slice.18
  570.5 0.3 reduce-window.9
  570.7 0.1 slice.181
  571.5 0.1 slice_reduce_fusion.16
  571.6 0.1 add_bitcast_fusion
  571.7 40.3 %reduce-scatter.2.cloned.1.call-done = bf16[16,1536]{1,0:T(8,128)(2,1)} async-done(((bf16[128,1536]{1,0:T(8,128)(2,1)}), bf16[16,1536]{1,0:T(8,128)(2,1)}) %reduce-scatter.2.cloned.1.call-update) | async-done | bytes 49168 | tf_op jit(solution)/shard_map/reduce_scatter | solution.py:173
  612.0 1.0 fusion.83
  613.0 0.7 multiply_reduce_fusion.1
  613.8 0.2 fusion.64
  614.0 0.1 constant_dynamic-slice_fusion
  614.1 7.4 %collective-permute-start = (f32[16,32]{1,0:T(8,128)S(1)}, f32[16,32]{1,0:T(8,128)S(1)}, u32[]{:S(2)}, u32[]{:S(2)}) collective-permute-start(f32[16,32]{1,0:T(8,128)S(1)} %constant_dynamic-slice_fusion), channel_id=1, source_target_pairs={{0,256},{256,0},{1,257},{257,1},{2,258},{258,2},{3,259},{259,3},{4... | collective-permute-start | bytes 6152 | tf_op jit(solution)/shard_map/ppermute | solution.py:19
  621.4 0.7 select_reduce_fusion
  625.6 0.0 collective-permute-done
  625.7 0.7 multiply_add_fusion.1
  (54 shorter events, 0.4 us)
Async XLA Ops:
  7.2 6.7 %copy-start = (bf16[3,192,1536]{2,1,0:T(8,128)(2,1)S(1)}, bf16[3,192,1536]{2,1,0:T(8,128)(2,1)}, u32[]{:S(2)}) copy-start(bf16[3,192,1536]{2,1,0:T(8,128)(2,1)} %param.16) | copy-start | bytes 5308420
  8.8 6.9 %copy-start.14 = (pred[128]{0:T(512)(128)(4,1)}, pred[128]{0:T(512)(128)(4,1)S(1)}, u32[]{:S(2)}) copy-start(pred[128]{0:T(512)(128)(4,1)S(1)} %get-tuple-element.46) | copy-start | bytes 388
  12.6 3.9 copy-start.16
  15.7 0.7 copy-start.4
  19.1 57.0 %all-to-all-start = ((bf16[32,128,192]{1,2,0:T(8,128)(2,1)}), bf16[32,128,192]{1,2,0:T(8,128)(2,1)S(1)}, u32[]{:S(2)}, u32[]{:S(2)}) async-start(bf16[32,128,192]{1,2,0:T(8,128)(2,1)} %stack.2), calls=%async_computation | async-start | bytes 3145728 | tf_op jit(solution)/shard_map/all_to_all | solution.py:125
  32.3 140.4 %all-gather.9.cloned.1.call-start = ((), (), s32[]{:S(2)}) async-start(), calls=%async_computation.6 | async-start | bytes 1622016 | tf_op jit(solution)/shard_map/all_gather | solution.py:127
  33.9 213.6 %all-reduce.3.cloned.1.call-start = ((), (), s32[]{:S(2)}) async-start(), calls=%async_computation.2 | async-start | bytes 786432 | tf_op jit(solution)/shard_map/psum | solution.py:159
  81.9 2.7 copy-start.1
  172.7 4.7 copy-start.3
  172.7 74.8 %copy-start.2 = (bf16[1,128,1536]{2,1,0:T(8,128)(2,1)S(1)}, bf16[1,128,1536]{2,1,0:T(8,128)(2,1)}, u32[]{:S(2)}) copy-start(bf16[1,128,1536]{2,1,0:T(8,128)(2,1)} %param.13) | copy-start | bytes 1179652
  172.7 74.8 %copy-start.15 = (pred[128]{0:T(512)(128)(4,1)S(1)}, pred[128]{0:T(512)(128)(4,1)}, u32[]{:S(2)}) copy-start(pred[128]{0:T(512)(128)(4,1)} %copy-done.14) | copy-start | bytes 388
  177.3 388.5 %copy-start.9 = (f32[1536]{0:T(1024)S(1)}, f32[1536]{0:T(1024)}, u32[]{:S(2)}) copy-start(f32[1536]{0:T(1024)} %get-tuple-element.18) | copy-start | bytes 18436
  177.3 388.5 %copy-start.10 = (f32[1536]{0:T(1024)S(1)}, f32[1536]{0:T(1024)}, u32[]{:S(2)}) copy-start(f32[1536]{0:T(1024)} %get-tuple-element.19) | copy-start | bytes 18436
  177.3 388.4 %copy-start.11 = (f32[1536]{0:T(1024)S(1)}, f32[1536]{0:T(1024)}, u32[]{:S(2)}) copy-start(f32[1536]{0:T(1024)} %get-tuple-element.20) | copy-start | bytes 18436
  177.3 388.4 %copy-start.12 = (f32[1536]{0:T(1024)S(1)}, f32[1536]{0:T(1024)}, u32[]{:S(2)}) copy-start(f32[1536]{0:T(1024)} %get-tuple-element.28) | copy-start | bytes 18436
  178.4 225.2 %all-gather.5.cloned.1.call-start = ((), (), s32[]{:S(2)}) async-start(), calls=%async_computation.3 | async-start | bytes 2433024 | tf_op jit(solution)/shard_map/all_gather | solution.py:167
  179.1 386.6 %all-gather.7.cloned.1.call-start = ((), (), s32[]{:S(2)}) async-start(), calls=%async_computation.4 | async-start | bytes 2433024 | tf_op jit(solution)/shard_map/all_gather | solution.py:168
  179.7 432.2 %reduce-scatter.2.cloned.1.call-start = ((), (), s32[]{:S(2)}) async-start(), calls=%async_computation.5 | async-start | bytes 442368 | tf_op jit(solution)/shard_map/reduce_scatter | solution.py:173
  565.7 48.0 %copy-start.5 = (f32[1536]{0:T(1024)S(1)}, f32[1536]{0:T(1024)}, u32[]{:S(2)}) copy-start(f32[1536]{0:T(1024)} %get-tuple-element.16) | copy-start | bytes 18436
  565.8 48.0 %copy-start.6 = (f32[1536]{0:T(1024)S(1)}, f32[1536]{0:T(1024)}, u32[]{:S(2)}) copy-start(f32[1536]{0:T(1024)} %get-tuple-element.17) | copy-start | bytes 18436
  565.8 48.0 %copy-start.7 = (f32[1536]{0:T(1024)S(1)}, f32[1536]{0:T(1024)}, u32[]{:S(2)}) copy-start(f32[1536]{0:T(1024)} %get-tuple-element.37) | copy-start | bytes 18436
  565.8 48.0 %copy-start.8 = (f32[1536]{0:T(1024)S(1)}, f32[1536]{0:T(1024)}, u32[]{:S(2)}) copy-start(f32[1536]{0:T(1024)} %get-tuple-element.38) | copy-start | bytes 18436
  565.8 48.0 %copy-start.17 = (bf16[1536,64]{0,1:T(8,128)(2,1)S(1)}, bf16[1536,64]{0,1:T(8,128)(2,1)}, u32[]{:S(2)}) copy-start(bf16[1536,64]{0,1:T(8,128)(2,1)} %param.20) | copy-start | bytes 589828
  565.8 59.8 %copy-start.13 = (f32[16,32]{1,0:T(8,128)S(1)}, f32[16,32]{1,0:T(8,128)}, u32[]{:S(2)}) copy-start(f32[16,32]{1,0:T(8,128)} %param.21) | copy-start | bytes 6148
  614.1 11.6 %collective-permute-start = (f32[16,32]{1,0:T(8,128)S(1)}, f32[16,32]{1,0:T(8,128)S(1)}, u32[]{:S(2)}, u32[]{:S(2)}) collective-permute-start(f32[16,32]{1,0:T(8,128)S(1)} %constant_dynamic-slice_fusion), channel_id=1, source_target_pairs={{0,256},{256,0},{1,257},{257,1},{2,258},{258,2},{3,259},{259,3},{4... | collective-permute-start | bytes 6152 | tf_op jit(solution)/shard_map/ppermute | solution.py:19
Sparse Core Ops, SparseCore 0:
  35.7 136.9 all-gather.8
  178.5 68.8 all-reduce.2
  249.7 153.8 all-gather.4
  405.7 159.9 all-gather.6
  570.5 41.4 reduce-scatter.1
